TPU v7x, 128 devices: a whole 4x4x4 slice. The times are simulated.
128 devices in a mesh: dp: 8 (over z, core), ctx: 16 (over y, x).
Axes of the slice: x: 4, y: 4, z: 4, core: 2. Of those that a mesh axis runs over, the one named last changes fastest.
Arguments:
- attn_in: bfloat16 [8, 2048, 4096], P('dp', 'ctx'), may hold values from -6 to 6
- attn_mix: bfloat16 [8, 2048, 4096], P('dp', 'ctx'), may hold values from -6 to 6
- mlp_in: bfloat16 [8, 2048, 4096], P('dp', 'ctx'), may hold values from -6 to 6
- mlp_act: bfloat16 [8, 2048, 14336], P('dp', 'ctx'), may hold values from -6 to 6
- grad_query: bfloat16 [8, 2048, 4096], P('dp', 'ctx'), may hold values from -0.19921875 to 0.19921875
- grad_key: bfloat16 [8, 2048, 1024], P('dp', 'ctx'), may hold values from -0.19921875 to 0.19921875
- grad_value: bfloat16 [8, 2048, 1024], P('dp', 'ctx'), may hold values from -0.19921875 to 0.19921875
- grad_output: bfloat16 [8, 2048, 4096], P('dp', 'ctx'), may hold values from -0.19921875 to 0.19921875
- grad_gate: bfloat16 [8, 2048, 14336], P('dp', 'ctx'), may hold values from -0.19921875 to 0.19921875
- grad_up: bfloat16 [8, 2048, 14336], P('dp', 'ctx'), may hold values from -0.19921875 to 0.19921875
- grad_down: bfloat16 [8, 2048, 4096], P('dp', 'ctx'), may hold values from -0.19921875 to 0.19921875
- proj_attn: bfloat16 [4096, 64], replicated, may hold values from -0.09375 to 0.09375
- proj_mix: bfloat16 [4096, 64], replicated, may hold values from -0.09375 to 0.09375
- proj_mlp: bfloat16 [4096, 64], replicated, may hold values from -0.09375 to 0.09375
- proj_act: bfloat16 [14336, 64], replicated, may hold values from -0.046875 to 0.046875
- proj_query: bfloat16 [4096, 64], replicated, may hold values from -0.09375 to 0.09375
- proj_key: bfloat16 [1024, 64], replicated, may hold values from -0.1875 to 0.1875
- proj_value: bfloat16 [1024, 64], replicated, may hold values from -0.1875 to 0.1875
- proj_output: bfloat16 [4096, 64], replicated, may hold values from -0.09375 to 0.09375
- proj_gate: bfloat16 [14336, 64], replicated, may hold values from -0.046875 to 0.046875
- proj_upward: bfloat16 [14336, 64], replicated, may hold values from -0.046875 to 0.046875
- proj_down: bfloat16 [4096, 64], replicated, may hold values from -0.09375 to 0.09375
- seq_counts: int32 [8], P('dp'), may hold values from 128 to 2048, as said below
- example_ids: int32 [8], replicated, may hold values from 0 to 7, each once
Outputs:
- store: float32 [8, 7, 4096], P('dp', None, 'ctx')
Inputs may be any that keep to these rules, and one draw needn't show every extreme that they name: `seq_counts`: every count is a multiple of 128; some sequence has all 2048 tokens. `example_ids`: a permutation: every store row receives exactly one sequence.
All inputs are finite; a program needn't handle non-finite values.
Results may differ from a plain program's by a relative error of at most 0.004.
Values sent between devices are 32-bit elements; how exact they have to be, the bound alone decides.
No kernel may reach another device: no remote copies, remote signals or barrier semaphores. Data moves between devices by JAX's collectives and lax.ppermute only.
A program may use at most 128 MiB of HBM per device.

v0:
```python
import jax
import jax.numpy as jnp
from jax import lax
from jax.sharding import PartitionSpec as P


def project_rows(acts, projection):
    return jnp.dot(acts[0], projection, preferred_element_type=jnp.float32).astype(jnp.bfloat16)


def outer_sum(grads_proj, inputs_proj):
    product = lax.dot_general(
        grads_proj, inputs_proj, (((0,), (0,)), ((), ())), preferred_element_type=jnp.float32
    )
    return product.reshape(-1)


def reduce_positions(values):
    summed = lax.psum(values, "ctx")
    width = values.shape[2] // lax.axis_size("ctx")
    return lax.dynamic_slice_in_dim(summed, lax.axis_index("ctx") * width, width, 2)


def pick_owned(gathered, example_ids):
    owner = lax.axis_index("dp")
    weights = (example_ids == owner).astype(jnp.float32)
    return jnp.sum(weights[:, None, None] * gathered, axis=0, keepdims=True)


def shards(
    attn_in,
    attn_mix,
    mlp_in,
    mlp_act,
    grad_query,
    grad_key,
    grad_value,
    grad_output,
    grad_gate,
    grad_up,
    grad_down,
    proj_attn,
    proj_mix,
    proj_mlp,
    proj_act,
    proj_query,
    proj_key,
    proj_value,
    proj_output,
    proj_gate,
    proj_upward,
    proj_down,
    seq_counts,
    example_ids,
):
    length_dev = attn_in.shape[1]
    first_pos = lax.axis_index("ctx") * length_dev
    limit_pos = seq_counts[0]
    live_rows = (first_pos + jnp.arange(length_dev, dtype=jnp.int32) < limit_pos).astype(
        jnp.bfloat16
    )[:, None]
    attn_p = project_rows(attn_in, proj_attn)
    mix_p = project_rows(attn_mix, proj_mix)
    mlp_p = project_rows(mlp_in, proj_mlp)
    act_p = project_rows(mlp_act, proj_act)
    pairs = [
        (grad_query, proj_query, attn_p),
        (grad_key, proj_key, attn_p),
        (grad_value, proj_value, attn_p),
        (grad_output, proj_output, mix_p),
        (grad_gate, proj_gate, mlp_p),
        (grad_up, proj_upward, mlp_p),
        (grad_down, proj_down, act_p),
    ]
    sketches = [
        outer_sum(project_rows(grads, projection) * live_rows, inputs_proj)
        for grads, projection, inputs_proj in pairs
    ]
    partial_sum = jnp.stack(sketches, axis=0)[None]
    shared = reduce_positions(partial_sum)
    gathered = lax.all_gather(shared, "dp", axis=0, tiled=True)
    return pick_owned(gathered, example_ids)


def solution(mesh):
    return jax.shard_map(
        shards,
        mesh=mesh,
        in_specs=(
            P("dp", "ctx", None),
            P("dp", "ctx", None),
            P("dp", "ctx", None),
            P("dp", "ctx", None),
            P("dp", "ctx", None),
            P("dp", "ctx", None),
            P("dp", "ctx", None),
            P("dp", "ctx", None),
            P("dp", "ctx", None),
            P("dp", "ctx", None),
            P("dp", "ctx", None),
            P(),
            P(),
            P(),
            P(),
            P(),
            P(),
            P(),
            P(),
            P(),
            P(),
            P(),
            P("dp"),
            P(),
        ),
        out_specs=P("dp", None, "ctx"),
        check_vma=False,
    )
```

profile of v0, /device:TPU:1, one launch (start us, length us, event | category | flops | bytes accessed | tf_op | source)
XLA Modules:
  0.0 140.8 jit_solution(12949452242620769150)
XLA Ops:
  6.5 0.0 copy-start
  6.5 0.0 all-reduce.2.cloned.1.call-start
  7.3 1.8 %convolution_convert_fusion.6 = bf16[128,64]{0,1:T(8,128)(2,1)S(1)} fusion(bf16[4096,64]{0,1:T(8,128)(2,1)} %param.37, bf16[1,128,4096]{2,1,0:T(8,128)(2,1)} %param.26), kind=kOutput, calls=%fused_computation.29 | convolution fusion | flops 67117056 | bytes 1589248 | tf_op jit(solution)/shard_map/dot_general | solution.py:8
  9.2 0.0 copy-done
  9.2 3.3 %fusion.22 = f32[64,64]{1,0:T(8,128)S(1)} fusion(bf16[128,64]{0,1:T(8,128)(2,1)S(1)} %convolution_convert_fusion.6, bf16[14336,64]{0,1:T(8,128)(2,1)S(1)} %copy-done, bf16[1,128,14336]{2,1,0:T(8,128)(2,1)} %param.33, bf16[128]{0:T(256)(128)(2,1)S(1)} %compare_convert_fusion), kind=kOutput, calls=%fused_computation.17 | convolution fusion | flops 235945984 | bytes 5538048 | tf_op jit(solution)/shard_map/dot_general | solution.py:12
  12.5 0.0 copy-start.2
  12.5 0.1 stack_reshape.26
  12.6 0.0 copy-start.1
  12.6 4.0 %fusion.28 = f32[64,64]{1,0:T(8,128)S(1)} fusion(bf16[128,64]{0,1:T(8,128)(2,1)S(1)} %convolution_convert_fusion.6, bf16[14336,64]{0,1:T(8,128)(2,1)} %param.43, bf16[1,128,14336]{2,1,0:T(8,128)(2,1)} %param.32, bf16[128]{0:T(256)(128)(2,1)S(1)} %compare_convert_fusion), kind=kOutput, calls=%fused_computation.19 | convolution fusion | flops 235945984 | bytes 5538048 | tf_op jit(solution)/shard_map/dot_general | solution.py:12
  16.6 0.1 stack_reshape.25
  16.7 0.0 copy-done.2
  16.7 1.7 %convolution_convert_fusion.7 = bf16[128,64]{0,1:T(8,128)(2,1)S(1)} fusion(bf16[4096,64]{0,1:T(8,128)(2,1)S(1)} %copy-done.2, bf16[1,128,4096]{2,1,0:T(8,128)(2,1)} %param.24), kind=kOutput, calls=%fused_computation.30 | convolution fusion | flops 67117056 | bytes 1589248 | tf_op jit(solution)/shard_map/dot_general | solution.py:8
  18.4 0.0 copy-start.3
  18.4 1.4 %fusion.38 = f32[64,64]{1,0:T(8,128)S(1)} fusion(bf16[128,64]{0,1:T(8,128)(2,1)S(1)} %convolution_convert_fusion.7, bf16[1024,64]{0,1:T(8,128)(2,1)} %param.41, bf16[1,128,1024]{2,1,0:T(8,128)(2,1)} %param.30, bf16[128]{0:T(256)(128)(2,1)S(1)} %compare_convert_fusion), kind=kOutput, calls=%fused_computation.28 | convolution fusion | flops 17842176 | bytes 426240 | tf_op jit(solution)/shard_map/dot_general | solution.py:12
  19.8 0.1 stack_reshape.23
  20.0 1.4 fusion.36
  21.3 0.1 stack_reshape.22
  21.4 0.0 copy-done.1
  21.4 1.6 %fusion.31 = f32[64,64]{1,0:T(8,128)S(1)} fusion(bf16[128,64]{0,1:T(8,128)(2,1)S(1)} %convolution_convert_fusion.7, bf16[4096,64]{0,1:T(8,128)(2,1)} %param.39, bf16[1,128,4096]{2,1,0:T(8,128)(2,1)S(1)} %copy-done.1, bf16[128]{0:T(256)(128)(2,1)S(1)} %compare_convert_fusion), kind=kOutput, calls=%fused_computation.21 | convolution fusion | flops 68173824 | bytes 1605888 | tf_op jit(solution)/shard_map/dot_general | solution.py:12
  23.1 0.1 stack_reshape.21
  23.2 1.8 %convolution_convert_fusion.1 = bf16[128,64]{1,0:T(8,128)(2,1)S(1)} fusion(bf16[4096,64]{0,1:T(8,128)(2,1)} %param.36, bf16[1,128,4096]{2,1,0:T(8,128)(2,1)} %param.25), kind=kOutput, calls=%fused_computation.10 | convolution fusion | flops 67117056 | bytes 1589248 | tf_op jit(solution)/shard_map/dot_general | solution.py:8
  25.0 0.0 copy-done.3
  25.0 1.8 %fusion.33 = f32[64,64]{1,0:T(8,128)S(1)} fusion(bf16[128,64]{1,0:T(8,128)(2,1)S(1)} %convolution_convert_fusion.1, bf16[4096,64]{0,1:T(8,128)(2,1)S(1)} %copy-done.3, bf16[1,128,4096]{2,1,0:T(8,128)(2,1)} %param.31, bf16[128]{0:T(256)(128)(2,1)S(1)} %compare_convert_fusion), kind=kOutput, calls=%fused_computation.23 | convolution fusion | flops 68173824 | bytes 1605888 | tf_op jit(solution)/shard_map/dot_general | solution.py:12
  26.8 0.1 stack_reshape.24
  26.9 0.0 copy-start.4
  26.9 1.8 %fusion.34 = bf16[128,64]{1,0:T(8,128)(2,1)S(1)} fusion(bf16[4096,64]{0,1:T(8,128)(2,1)} %param.45, bf16[1,128,4096]{2,1,0:T(8,128)(2,1)} %param.34, bf16[128]{0:T(256)(128)(2,1)S(1)} %compare_convert_fusion), kind=kOutput, calls=%fused_computation.24 | convolution fusion | flops 67125248 | bytes 1589504 | tf_op jit(solution)/shard_map/dot_general | solution.py:8
  28.7 3.8 %fusion.16 = f32[64,64]{1,0:T(8,128)S(1)} fusion(bf16[128,64]{1,0:T(8,128)(2,1)S(1)} %fusion.34, bf16[14336,64]{0,1:T(8,128)(2,1)} %param.38, bf16[1,128,14336]{2,1,0:T(8,128)(2,1)} %param.27), kind=kOutput, calls=%fused_computation.15 | convolution fusion | flops 235937792 | bytes 5537792 | tf_op jit(solution)/shard_map/dot_general | solution.py:12
  32.5 0.1 stack_reshape.27
  32.6 0.8 stack.3
  33.4 0.0 all-reduce.2.cloned.1.call-update
  33.5 0.0 copy-done.4
  33.5 83.8 %all-reduce.2.cloned.1.call-done = f32[1,7,4096]{2,1,0:T(8,128)} async-done(((f32[1,7,4096]{2,1,0:T(8,128)}), f32[1,7,4096]{2,1,0:T(8,128)}) %all-reduce.2.cloned.1.call-update) | async-done | bytes 114704 | tf_op jit(solution)/shard_map/psum | solution.py:19
  117.3 0.7 constant_dynamic-slice_fusion
  118.0 15.2 %all_gather.3 = f32[8,7,256]{2,1,0:T(8,128)S(1)} all-gather(f32[1,7,256]{2,1,0:T(8,128)S(1)} %constant_dynamic-slice_fusion), channel_id=1, replica_groups=mesh['dp'=8,'ctx'=16] {'dp'}, dimensions={0}, use_global_device_ids=true | all-gather | bytes 64512 | tf_op jit(solution)/shard_map/all_gather | solution.py:81
  133.3 0.1 multiply_reduce_fusion
  133.3 0.6 broadcast_in_dim.9
  (2 shorter events, 0.0 us)
Async XLA Ops:
  6.5 2.7 %copy-start = (bf16[14336,64]{0,1:T(8,128)(2,1)S(1)}, bf16[14336,64]{0,1:T(8,128)(2,1)}, u32[]{:S(2)}) copy-start(bf16[14336,64]{0,1:T(8,128)(2,1)} %param.44) | copy-start | bytes 5505028
  6.5 110.8 %all-reduce.2.cloned.1.call-start = ((), (), s32[]{:S(2)}) async-start(), calls=%async_computation | async-start | bytes 262144 | tf_op jit(solution)/shard_map/psum | solution.py:19
  12.5 4.2 %copy-start.2 = (bf16[4096,64]{0,1:T(8,128)(2,1)S(1)}, bf16[4096,64]{0,1:T(8,128)(2,1)}, u32[]{:S(2)}) copy-start(bf16[4096,64]{0,1:T(8,128)(2,1)} %param.35) | copy-start | bytes 1572868
  12.6 8.8 %copy-start.1 = (bf16[1,128,4096]{2,1,0:T(8,128)(2,1)S(1)}, bf16[1,128,4096]{2,1,0:T(8,128)(2,1)}, u32[]{:S(2)}) copy-start(bf16[1,128,4096]{2,1,0:T(8,128)(2,1)} %param.28) | copy-start | bytes 3145732
  18.4 6.6 %copy-start.3 = (bf16[4096,64]{0,1:T(8,128)(2,1)S(1)}, bf16[4096,64]{0,1:T(8,128)(2,1)}, u32[]{:S(2)}) copy-start(bf16[4096,64]{0,1:T(8,128)(2,1)} %param.42) | copy-start | bytes 1572868
  26.9 6.6 %copy-start.4 = (s32[8]{0:T(128)S(1)}, s32[8]{0:T(128)}, u32[]{:S(2)}) copy-start(s32[8]{0:T(128)} %param.47) | copy-start | bytes 100
Sparse Core Ops, SparseCore 0:
  33.6 83.6 all-reduce.1
where the time goes:
time: 141 us
  waiting for transfers between devices  83.8 us (59%)
  matrix products  24.4 us (17%)
  blocking collectives  15.2 us (11%)
  between operations  14.3 us (10%)
  local copies, waits for them, and re-layouts  2.84 us (2%)
    psum x1, waiting for transfers between devices, reduce_positions(): summed = lax.psum(values, 'ctx')  83.8 us
    dot_general x7, matrix products, outer_sum(): lax.dot_general(grads_proj, inputs_proj, (((0,), (0,)), ((), ())), prefer...  17.3 us
    all_gather x1, blocking collectives, shards(): gathered = lax.all_gather(shared, 'dp', axis=0, tiled=True)  15.2 us
    dot_general x4, matrix products, project_rows(): jnp.dot(acts[0], projection, preferred_element_type=jnp.float32)  7.1 us
  transfers between devices with their start and end apart: 1, of which 1 were waited for; matrix products, arithmetic and copies ran while one was open for 0% of the time, Pallas kernels for 0%

commit v1 on v0

--- a/solution.py
+++ b/solution.py
@@ -2,6 +2,23 @@
 import jax.numpy as jnp
 from jax import lax
 from jax.sharding import PartitionSpec as P
+
+
+def _raise_skins(row_data):
+    count_all = lax.axis_size("ctx")
+
+    def raise_stocks(formed, passed):
+        if passed >= count_all:
+            return formed
+        pieces_in = []
+        for t in range(count_all):
+            pieces_in.append((t, t ^ passed))
+        near = lax.ppermute(formed, "ctx", pieces_in)
+        taken_in = raise_stocks(formed + near, 2 * passed)
+        return taken_in
+
+    z_new = raise_stocks(row_data, 1)
+    return z_new
 
 
 def project_rows(acts, projection):
@@ -16,7 +33,7 @@
 
 
 def reduce_positions(values):
-    summed = lax.psum(values, "ctx")
+    summed = _raise_skins(values)
     width = values.shape[2] // lax.axis_size("ctx")
     return lax.dynamic_slice_in_dim(summed, lax.axis_index("ctx") * width, width, 2)
 

time: 141 us -> 66.5 us (0.47)
  waiting for transfers between devices: 83.8 us -> 10.9 us
  between operations: 14.3 us -> 0.96 us
  starting transfers between devices: 0.01 us -> 10.1 us
  blocking collectives: 15.2 us -> 17.6 us
    psum x1 -> x0, waiting for transfers between devices: 83.8 us -> none  [reduce_positions(): summed = lax.psum(values, 'ctx')]
    ppermute x0 -> x4, waiting for transfers between devices: none -> 10.9 us  [raise_stocks(): near = lax.ppermute(formed, 'ctx', pieces_in)]
    ppermute x0 -> x4, starting transfers between devices: none -> 10.1 us  [raise_stocks(): near = lax.ppermute(formed, 'ctx', pieces_in)]
    all_gather x1, blocking collectives: 15.2 us -> 17.6 us  [shards(): gathered = lax.all_gather(shared, 'dp', axis=0, tiled=True)]
  transfers between devices with their start and end apart: 1 -> 4, of which waited for: 1 -> 4; matrix products, arithmetic and copies ran while one was open for 0% -> 0% of each run, Pallas kernels for 0% -> 0%
where the time goes in v1:
time: 66.5 us; the launch traced here: 65.8 us
  matrix products  24.4 us (37%)
  blocking collectives  17.6 us (26%)
  waiting for transfers between devices  10.9 us (16%)
  starting transfers between devices  10.1 us (15%)
  local copies, waits for them, and re-layouts  1.51 us (2%)
  between operations  0.96 us (1%)
    all_gather x1, blocking collectives, shards(): gathered = lax.all_gather(shared, 'dp', axis=0, tiled=True)  17.6 us
    dot_general x7, matrix products, outer_sum(): lax.dot_general(grads_proj, inputs_proj, (((0,), (0,)), ((), ())), prefer...  17.3 us
    ppermute x4, waiting for transfers between devices, raise_stocks(): near = lax.ppermute(formed, 'ctx', pieces_in)  10.9 us
    ppermute x4, starting transfers between devices, raise_stocks(): near = lax.ppermute(formed, 'ctx', pieces_in)  10.1 us
    dot_general x4, matrix products, project_rows(): jnp.dot(acts[0], projection, preferred_element_type=jnp.float32)  7.1 us
  transfers between devices with their start and end apart: 4, of which 4 were waited for; matrix products, arithmetic and copies ran while one was open for 0% of the time, Pallas kernels for 0%

profile of v1, /device:TPU:1, one launch (start us, length us, event | category | flops | bytes accessed | tf_op | source)
XLA Modules:
  0.0 65.8 jit_solution(2322433838614786543)
XLA Ops:
  0.0 0.0 copy-start
  0.8 1.8 %convolution_convert_fusion.6 = bf16[128,64]{0,1:T(8,128)(2,1)S(1)} fusion(bf16[4096,64]{0,1:T(8,128)(2,1)} %param.37, bf16[1,128,4096]{2,1,0:T(8,128)(2,1)} %param.26), kind=kOutput, calls=%fused_computation.29 | convolution fusion | flops 67117056 | bytes 1589248 | tf_op jit(solution)/shard_map/dot_general | solution.py:25
  2.6 0.0 copy-done
  2.7 3.3 %fusion.22 = f32[64,64]{1,0:T(8,128)S(1)} fusion(bf16[128,64]{0,1:T(8,128)(2,1)S(1)} %convolution_convert_fusion.6, bf16[14336,64]{0,1:T(8,128)(2,1)S(1)} %copy-done, bf16[1,128,14336]{2,1,0:T(8,128)(2,1)} %param.33, bf16[128]{0:T(256)(128)(2,1)S(1)} %compare_convert_fusion), kind=kOutput, calls=%fused_computation.17 | convolution fusion | flops 235945984 | bytes 5538048 | tf_op jit(solution)/shard_map/dot_general | solution.py:29
  6.0 0.0 copy-start.2
  6.0 0.1 stack_reshape.26
  6.1 0.0 copy-start.1
  6.1 4.0 %fusion.28 = f32[64,64]{1,0:T(8,128)S(1)} fusion(bf16[128,64]{0,1:T(8,128)(2,1)S(1)} %convolution_convert_fusion.6, bf16[14336,64]{0,1:T(8,128)(2,1)} %param.43, bf16[1,128,14336]{2,1,0:T(8,128)(2,1)} %param.32, bf16[128]{0:T(256)(128)(2,1)S(1)} %compare_convert_fusion), kind=kOutput, calls=%fused_computation.19 | convolution fusion | flops 235945984 | bytes 5538048 | tf_op jit(solution)/shard_map/dot_general | solution.py:29
  10.0 0.1 stack_reshape.25
  10.2 0.0 copy-done.2
  10.2 1.7 %convolution_convert_fusion.7 = bf16[128,64]{0,1:T(8,128)(2,1)S(1)} fusion(bf16[4096,64]{0,1:T(8,128)(2,1)S(1)} %copy-done.2, bf16[1,128,4096]{2,1,0:T(8,128)(2,1)} %param.24), kind=kOutput, calls=%fused_computation.30 | convolution fusion | flops 67117056 | bytes 1589248 | tf_op jit(solution)/shard_map/dot_general | solution.py:25
  11.9 0.0 copy-start.3
  11.9 1.4 %fusion.38 = f32[64,64]{1,0:T(8,128)S(1)} fusion(bf16[128,64]{0,1:T(8,128)(2,1)S(1)} %convolution_convert_fusion.7, bf16[1024,64]{0,1:T(8,128)(2,1)} %param.41, bf16[1,128,1024]{2,1,0:T(8,128)(2,1)} %param.30, bf16[128]{0:T(256)(128)(2,1)S(1)} %compare_convert_fusion), kind=kOutput, calls=%fused_computation.28 | convolution fusion | flops 17842176 | bytes 426240 | tf_op jit(solution)/shard_map/dot_general | solution.py:29
  13.3 0.1 stack_reshape.23
  13.4 1.4 %fusion.36 = f32[64,64]{1,0:T(8,128)S(1)} fusion(bf16[128,64]{0,1:T(8,128)(2,1)S(1)} %convolution_convert_fusion.7, bf16[1024,64]{0,1:T(8,128)(2,1)} %param.40, bf16[1,128,1024]{2,1,0:T(8,128)(2,1)} %param.29, bf16[128]{0:T(256)(128)(2,1)S(1)} %compare_convert_fusion), kind=kOutput, calls=%fused_computation.26 | convolution fusion | flops 17842176 | bytes 426240 | tf_op jit(solution)/shard_map/dot_general | solution.py:29
  14.8 0.1 stack_reshape.22
  14.9 0.0 copy-done.1
  14.9 1.6 %fusion.31 = f32[64,64]{1,0:T(8,128)S(1)} fusion(bf16[128,64]{0,1:T(8,128)(2,1)S(1)} %convolution_convert_fusion.7, bf16[4096,64]{0,1:T(8,128)(2,1)} %param.39, bf16[1,128,4096]{2,1,0:T(8,128)(2,1)S(1)} %copy-done.1, bf16[128]{0:T(256)(128)(2,1)S(1)} %compare_convert_fusion), kind=kOutput, calls=%fused_computation.21 | convolution fusion | flops 68173824 | bytes 1605888 | tf_op jit(solution)/shard_map/dot_general | solution.py:29
  16.5 0.1 stack_reshape.21
  16.6 1.8 %convolution_convert_fusion.1 = bf16[128,64]{1,0:T(8,128)(2,1)S(1)} fusion(bf16[4096,64]{0,1:T(8,128)(2,1)} %param.36, bf16[1,128,4096]{2,1,0:T(8,128)(2,1)} %param.25), kind=kOutput, calls=%fused_computation.10 | convolution fusion | flops 67117056 | bytes 1589248 | tf_op jit(solution)/shard_map/dot_general | solution.py:25
  18.4 0.0 copy-done.3
  18.4 1.8 %fusion.33 = f32[64,64]{1,0:T(8,128)S(1)} fusion(bf16[128,64]{1,0:T(8,128)(2,1)S(1)} %convolution_convert_fusion.1, bf16[4096,64]{0,1:T(8,128)(2,1)S(1)} %copy-done.3, bf16[1,128,4096]{2,1,0:T(8,128)(2,1)} %param.31, bf16[128]{0:T(256)(128)(2,1)S(1)} %compare_convert_fusion), kind=kOutput, calls=%fused_computation.23 | convolution fusion | flops 68173824 | bytes 1605888 | tf_op jit(solution)/shard_map/dot_general | solution.py:29
  20.2 0.1 stack_reshape.24
  20.4 1.8 %fusion.34 = bf16[128,64]{1,0:T(8,128)(2,1)S(1)} fusion(bf16[4096,64]{0,1:T(8,128)(2,1)} %param.45, bf16[1,128,4096]{2,1,0:T(8,128)(2,1)} %param.34, bf16[128]{0:T(256)(128)(2,1)S(1)} %compare_convert_fusion), kind=kOutput, calls=%fused_computation.24 | convolution fusion | flops 67125248 | bytes 1589504 | tf_op jit(solution)/shard_map/dot_general | solution.py:25
  22.1 0.0 copy-start.4
  22.2 3.8 %fusion.16 = f32[64,64]{1,0:T(8,128)S(1)} fusion(bf16[128,64]{1,0:T(8,128)(2,1)S(1)} %fusion.34, bf16[14336,64]{0,1:T(8,128)(2,1)} %param.38, bf16[1,128,14336]{2,1,0:T(8,128)(2,1)} %param.27), kind=kOutput, calls=%fused_computation.15 | convolution fusion | flops 235937792 | bytes 5537792 | tf_op jit(solution)/shard_map/dot_general | solution.py:29
  26.0 0.1 stack_reshape.27
  26.1 0.2 stack.3
  26.3 2.1 %collective-permute-start = (f32[1,7,4096]{2,1,0:T(8,128)S(1)}, f32[1,7,4096]{2,1,0:T(8,128)S(1)}, u32[]{:S(2)}, u32[]{:S(2)}) collective-permute-start(f32[1,7,4096]{2,1,0:T(8,128)S(1)} %bitcast.75), channel_id=1, source_target_pairs={{0,1},{1,0},{2,3},{3,2},{4,5},{5,4},{6,7},{7,6},{8,9},{9,8},{10,11... | collective-permute-start | bytes 344072 | tf_op jit(solution)/shard_map/ppermute | solution.py:16
  28.4 2.7 %collective-permute-done = f32[1,7,4096]{2,1,0:T(8,128)S(1)} collective-permute-done((f32[1,7,4096]{2,1,0:T(8,128)S(1)}, f32[1,7,4096]{2,1,0:T(8,128)S(1)}, u32[]{:S(2)}, u32[]{:S(2)}) %collective-permute-start) | collective-permute-done | bytes 114720 | tf_op jit(solution)/shard_map/ppermute | solution.py:16
  31.1 3.3 %collective-permute-start.1 = (f32[1,7,4096]{2,1,0:T(8,128)S(1)}, f32[1,7,4096]{2,1,0:T(8,128)S(1)}, u32[]{:S(2)}, u32[]{:S(2)}) collective-permute-start(f32[1,7,4096]{2,1,0:T(8,128)S(1)} %bitcast_add_fusion), channel_id=1, source_target_pairs={{0,2},{1,3},{2,0},{3,1},{4,6},{5,7},{6,4},{7,5},{8,10},{9,11},{10,... | collective-permute-start | bytes 344072 | tf_op jit(solution)/shard_map/ppermute | solution.py:16
  34.4 2.4 %collective-permute-done.1 = f32[1,7,4096]{2,1,0:T(8,128)S(1)} collective-permute-done((f32[1,7,4096]{2,1,0:T(8,128)S(1)}, f32[1,7,4096]{2,1,0:T(8,128)S(1)}, u32[]{:S(2)}, u32[]{:S(2)}) %collective-permute-start.1) | collective-permute-done | bytes 114720 | tf_op jit(solution)/shard_map/ppermute | solution.py:16
  36.8 1.6 %collective-permute-start.2 = (f32[1,7,4096]{2,1,0:T(8,128)S(1)}, f32[1,7,4096]{2,1,0:T(8,128)S(1)}, u32[]{:S(2)}, u32[]{:S(2)}) collective-permute-start(f32[1,7,4096]{2,1,0:T(8,128)S(1)} %add.28), channel_id=1, source_target_pairs={{0,4},{1,5},{2,6},{3,7},{4,0},{5,1},{6,2},{7,3},{8,12},{9,13},{10,... | collective-permute-start | bytes 344072 | tf_op jit(solution)/shard_map/ppermute | solution.py:16
  38.4 2.4 %collective-permute-done.2 = f32[1,7,4096]{2,1,0:T(8,128)S(1)} collective-permute-done((f32[1,7,4096]{2,1,0:T(8,128)S(1)}, f32[1,7,4096]{2,1,0:T(8,128)S(1)}, u32[]{:S(2)}, u32[]{:S(2)}) %collective-permute-start.2) | collective-permute-done | bytes 114720 | tf_op jit(solution)/shard_map/ppermute | solution.py:16
  40.7 3.2 %collective-permute-start.3 = (f32[1,7,4096]{2,1,0:T(8,128)S(1)}, f32[1,7,4096]{2,1,0:T(8,128)S(1)}, u32[]{:S(2)}, u32[]{:S(2)}) collective-permute-start(f32[1,7,4096]{2,1,0:T(8,128)S(1)} %add.29), channel_id=1, source_target_pairs={{0,8},{1,9},{2,10},{3,11},{4,12},{5,13},{6,14},{7,15},{8,0},{9,1},... | collective-permute-start | bytes 344072 | tf_op jit(solution)/shard_map/ppermute | solution.py:16
  43.9 0.0 copy-done.4
  43.9 3.5 %collective-permute-done.3 = f32[1,7,4096]{2,1,0:T(8,128)S(1)} collective-permute-done((f32[1,7,4096]{2,1,0:T(8,128)S(1)}, f32[1,7,4096]{2,1,0:T(8,128)S(1)}, u32[]{:S(2)}, u32[]{:S(2)}) %collective-permute-start.3) | collective-permute-done | bytes 114720 | tf_op jit(solution)/shard_map/ppermute | solution.py:16
  47.4 17.6 %all_gather.3 = f32[8,7,256]{2,1,0:T(8,128)S(1)} all-gather(f32[1,7,256]{2,1,0:T(8,128)S(1)} %dynamic-slice_add_fusion), channel_id=1, replica_groups=mesh['dp'=8,'ctx'=16] {'dp'}, dimensions={0}, use_global_device_ids=true | all-gather | bytes 64512 | tf_op jit(solution)/shard_map/all_gather | solution.py:98
  65.1 0.1 multiply_reduce_fusion
  65.1 0.6 broadcast_in_dim.9
  (6 shorter events, 0.1 us)
Async XLA Ops:
  0.0 2.6 %copy-start = (bf16[14336,64]{0,1:T(8,128)(2,1)S(1)}, bf16[14336,64]{0,1:T(8,128)(2,1)}, u32[]{:S(2)}) copy-start(bf16[14336,64]{0,1:T(8,128)(2,1)} %param.44) | copy-start | bytes 5505028
  6.0 4.2 %copy-start.2 = (bf16[4096,64]{0,1:T(8,128)(2,1)S(1)}, bf16[4096,64]{0,1:T(8,128)(2,1)}, u32[]{:S(2)}) copy-start(bf16[4096,64]{0,1:T(8,128)(2,1)} %param.35) | copy-start | bytes 1572868
  6.1 8.8 %copy-start.1 = (bf16[1,128,4096]{2,1,0:T(8,128)(2,1)S(1)}, bf16[1,128,4096]{2,1,0:T(8,128)(2,1)}, u32[]{:S(2)}) copy-start(bf16[1,128,4096]{2,1,0:T(8,128)(2,1)} %param.28) | copy-start | bytes 3145732
  11.9 6.6 %copy-start.3 = (bf16[4096,64]{0,1:T(8,128)(2,1)S(1)}, bf16[4096,64]{0,1:T(8,128)(2,1)}, u32[]{:S(2)}) copy-start(bf16[4096,64]{0,1:T(8,128)(2,1)} %param.42) | copy-start | bytes 1572868
  22.1 21.8 %copy-start.4 = (s32[8]{0:T(128)S(1)}, s32[8]{0:T(128)}, u32[]{:S(2)}) copy-start(s32[8]{0:T(128)} %param.47) | copy-start | bytes 100
  26.3 4.8 %collective-permute-start = (f32[1,7,4096]{2,1,0:T(8,128)S(1)}, f32[1,7,4096]{2,1,0:T(8,128)S(1)}, u32[]{:S(2)}, u32[]{:S(2)}) collective-permute-start(f32[1,7,4096]{2,1,0:T(8,128)S(1)} %bitcast.75), channel_id=1, source_target_pairs={{0,1},{1,0},{2,3},{3,2},{4,5},{5,4},{6,7},{7,6},{8,9},{9,8},{10,11... | collective-permute-start | bytes 344072 | tf_op jit(solution)/shard_map/ppermute | solution.py:16
  31.1 5.6 %collective-permute-start.1 = (f32[1,7,4096]{2,1,0:T(8,128)S(1)}, f32[1,7,4096]{2,1,0:T(8,128)S(1)}, u32[]{:S(2)}, u32[]{:S(2)}) collective-permute-start(f32[1,7,4096]{2,1,0:T(8,128)S(1)} %bitcast_add_fusion), channel_id=1, source_target_pairs={{0,2},{1,3},{2,0},{3,1},{4,6},{5,7},{6,4},{7,5},{8,10},{9,11},{10,... | collective-permute-start | bytes 344072 | tf_op jit(solution)/shard_map/ppermute | solution.py:16
  36.8 3.9 %collective-permute-start.2 = (f32[1,7,4096]{2,1,0:T(8,128)S(1)}, f32[1,7,4096]{2,1,0:T(8,128)S(1)}, u32[]{:S(2)}, u32[]{:S(2)}) collective-permute-start(f32[1,7,4096]{2,1,0:T(8,128)S(1)} %add.28), channel_id=1, source_target_pairs={{0,4},{1,5},{2,6},{3,7},{4,0},{5,1},{6,2},{7,3},{8,12},{9,13},{10,... | collective-permute-start | bytes 344072 | tf_op jit(solution)/shard_map/ppermute | solution.py:16
  40.7 6.7 %collective-permute-start.3 = (f32[1,7,4096]{2,1,0:T(8,128)S(1)}, f32[1,7,4096]{2,1,0:T(8,128)S(1)}, u32[]{:S(2)}, u32[]{:S(2)}) collective-permute-start(f32[1,7,4096]{2,1,0:T(8,128)S(1)} %add.29), channel_id=1, source_target_pairs={{0,8},{1,9},{2,10},{3,11},{4,12},{5,13},{6,14},{7,15},{8,0},{9,1},... | collective-permute-start | bytes 344072 | tf_op jit(solution)/shard_map/ppermute | solution.py:16
